TPU v7x, 32 devices: a whole 2x2x4 slice. The times are simulated.
32 devices in a mesh: groups: 2 (over y), owner: 8 (over z, core), tp: 2 (over x).
Axes of the slice: x: 2, y: 2, z: 4, core: 2. Of those that a mesh axis runs over, the one named last changes fastest.
Arguments:
- tokens: bfloat16 [8192, 8192], P(('groups', 'owner'), 'tp'), parts along dimension 0, may hold values from -6 to 6
- base_value_weight: bfloat16 [8192, 1024], P(('tp', 'owner')), may hold values from -0.0625 to 0.0625
- adapter_down_factor: bfloat16 [8, 8192, 64], P(None, ('tp', 'owner')), may hold values from -0.0625 to 0.0625
- adapter_up_factor: bfloat16 [8, 64, 1024], P(None, 'owner', 'tp'), may hold values from -0.75 to 0.75
- relevance_weight: float32 [1024], P('tp'), may hold values from -0.1875 to 0.1875
- tile_adapter_index: int32 [64], P(('groups', 'owner')), parts along dimension 0, may hold values from 0 to 7
- adapter_storage_slot: int32 [8], replicated, may hold values from 0 to 7, each once
- tile_live_length: int32 [64], P(('groups', 'owner')), parts along dimension 0, may hold values from 1 to 128, 3072 in all
- passage_document: int32 [64], P(('groups', 'owner')), parts along dimension 0, may hold values from 0 to 15, never falling along the last dimension, each value on 1 to 4 neighbouring positions
- document_output_slot: int32 [32], P('groups'), parts along dimension 0, may hold values from 0 to 15, each once
Outputs:
- values: bfloat16 [8192, 1024], P(('groups', 'owner'), 'tp'), parts along dimension 0
- doc_scores: float32 [32], P(('groups', 'owner')), parts along dimension 0
There are 2 independent parts, one for each index of `groups`. A program takes and returns all parts, laid end to end along the dimension named above; an argument that names none is the same for every part. Nothing has to cross between parts.
All inputs are finite; a program needn't handle non-finite values. No bound on the sum of `tile_live_length` on one device may be relied on, other than what follows from the above.
Results may differ from a plain program's by a relative error of at most 0.0039.
Values may be sent and summed in bfloat16 or wider, within the bound.
A program may use at most 64 MiB of HBM per device.

v0:
```python
import jax
import jax.numpy as jnp
from jax import lax
from jax.sharding import PartitionSpec as P

TILE = 128


def shards(
    tokens,
    base_value_weight,
    adapter_down_factor,
    adapter_up_factor,
    relevance_weight,
    tile_adapter_index,
    adapter_storage_slot,
    tile_live_length,
    passage_document,
    document_output_slot,
):
    n_owner = lax.axis_size("owner")
    owner_pos = lax.axis_index("owner")
    tok_dev, local_feat = tokens.shape
    tiles_dev = tok_dev // TILE
    adapters = adapter_storage_slot.shape[0]
    adapter_rank_width = adapter_down_factor.shape[2]
    value_local_width = adapter_up_factor.shape[2]
    docs = document_output_slot.shape[0]
    doc_dev = docs // n_owner
    my_slots = jnp.sum(
        jnp.where(
            tile_adapter_index[:, None] == jnp.arange(adapters, dtype=jnp.int32)[None, :],
            adapter_storage_slot[None, :],
            0,
        ),
        axis=1,
    )
    all_slots = lax.all_gather(my_slots, "owner", axis=0, tiled=True)
    requested_output = all_slots.reshape(n_owner, tiles_dev).T
    down_projected = adapter_down_factor[requested_output]
    down_in = lax.all_to_all(down_projected, "owner", split_axis=1, concat_axis=1, tiled=True)
    alternate_rows = lax.all_gather(adapter_up_factor, "owner", axis=1, tiled=True)
    picker = (my_slots[:, None] == jnp.arange(adapters, dtype=jnp.int32)[None, :]).astype(
        jnp.bfloat16
    )
    second = jnp.einsum(
        "ja,ark->jrk", picker, alternate_rows, preferred_element_type=jnp.float32
    ).astype(jnp.bfloat16)
    first_rows = down_in.reshape(tiles_dev, local_feat, adapter_rank_width)
    token_tiles = tokens.reshape(tiles_dev, TILE, local_feat)
    low_part = jnp.einsum(
        "jtf,jfr->jtr", token_tiles, first_rows, preferred_element_type=jnp.float32
    ).reshape(tok_dev, adapter_rank_width)
    partial_base = jnp.dot(
        tokens,
        lax.all_gather(base_value_weight, "owner", axis=0, tiled=True),
        preferred_element_type=jnp.float32,
    )
    base_share = lax.psum_scatter(partial_base, "tp", scatter_dimension=1, tiled=True)
    low_rank = lax.psum(low_part, "tp").astype(jnp.bfloat16)
    low_tiles = low_rank.reshape(tiles_dev, TILE, adapter_rank_width)
    adapter_term = jnp.einsum("jtr,jrk->jtk", low_tiles, second, preferred_element_type=jnp.float32)
    adapted = base_share + adapter_term.reshape(tok_dev, value_local_width)
    values = adapted.astype(jnp.bfloat16)
    token_part = jnp.dot(
        jax.nn.silu(adapted), relevance_weight, precision=lax.Precision.HIGHEST
    ).reshape(tiles_dev, TILE)
    live_mask = jnp.arange(TILE, dtype=jnp.int32)[None, :] < tile_live_length[:, None]
    passage_part = jnp.sum(jnp.where(live_mask, token_part, 0.0), axis=1)
    passage = lax.psum(passage_part, "tp") / jnp.sqrt(tile_live_length.astype(jnp.float32))
    doc_slot = jnp.sum(
        jnp.where(
            passage_document[:, None] == jnp.arange(docs, dtype=jnp.int32)[None, :],
            document_output_slot[None, :],
            0,
        ),
        axis=1,
    )
    candidate = jnp.max(
        jnp.where(
            doc_slot[:, None] == jnp.arange(docs, dtype=jnp.int32)[None, :], passage[:, None], -1e30
        ),
        axis=0,
    )
    merged = lax.pmax(candidate, "owner")
    doc_scores = lax.dynamic_slice_in_dim(merged, owner_pos * doc_dev, doc_dev, 0)
    return (values, doc_scores)


def solution(mesh):
    placed = (
        P(("groups", "owner"), "tp"),
        P(("tp", "owner"), None),
        P(None, ("tp", "owner"), None),
        P(None, "owner", "tp"),
        P("tp"),
        P(("groups", "owner")),
        P(),
        P(("groups", "owner")),
        P(("groups", "owner")),
        P("groups"),
    )
    return jax.shard_map(
        shards,
        mesh=mesh,
        in_specs=placed,
        out_specs=(P(("groups", "owner"), "tp"), P(("groups", "owner"))),
        check_vma=False,
    )
```

profile of v0, /device:TPU:0, one launch (start us, length us, event | category | flops | bytes accessed | tf_op | source)
XLA Modules:
  0.0 213.9 jit_solution(2184129054824787035)
XLA Ops:
  7.2 0.0 all-gather.2.cloned.1.call-start
  7.2 0.7 all-gather.2.cloned.1.call-update
  7.9 1.2 dynamic-slice
  9.8 0.8 select_reduce_fusion
  10.6 0.2 dynamic-update-slice
  10.8 10.6 %all-reduce = s32[32]{0:T(128)S(1)} all-reduce(s32[32]{0:T(128)S(1)} %dynamic-update-slice), channel_id=1, replica_groups=mesh['groups'=2,'owner'=8,'tp'=2] {'owner'}, use_global_device_ids=true, to_apply=%add | all-reduce | flops 32 | bytes 256
  21.4 0.1 reshape.33
  21.5 0.1 copy.38
  21.6 0.1 reshape.42
  21.7 0.7 gather_fusion
  22.4 1.4 copy.39
  23.8 3.6 %all-to-all-start = ((bf16[4,8,512,64]{2,3,0,1:T(8,128)(2,1)}), bf16[4,8,512,64]{2,3,0,1:T(8,128)(2,1)S(1)}, u32[]{:S(2)}, u32[]{:S(2)}) async-start(bf16[4,8,512,64]{2,3,0,1:T(8,128)(2,1)} %copy.39), calls=%async_computation.1 | async-start | bytes 4194304 | tf_op jit(solution)/shard_map/all_to_all | solution.py:41
  27.5 0.0 reduce-scatter.2.cloned.1.call-start
  27.5 111.4 %all-gather.2.cloned.1.call-done = bf16[4096,1024]{1,0:T(8,128)(2,1)} async-done(((bf16[512,1024]{1,0:T(8,128)(2,1)}), bf16[4096,1024]{1,0:T(8,128)(2,1)}) %all-gather.2.cloned.1.call-update) | async-done | bytes 8388624 | tf_op jit(solution)/shard_map/all_gather | solution.py:56
  138.9 10.5 %fusion.16 = f32[512,1024]{1,0:T(8,128)} fusion(bf16[512,4096]{1,0:T(8,128)(2,1)} %param.10, bf16[4096,1024]{1,0:T(8,128)(2,1)} %all-gather.2.cloned.1.call-done), kind=kOutput, calls=%fused_computation.33 | convolution fusion | flops 4294967296 | bytes 14680064 | tf_op jit(solution)/shard_map/dot_general | solution.py:54
  149.4 0.0 reduce-scatter.2.cloned.1.call-update
  149.5 0.2 select_reduce_fusion.3
  149.7 14.8 %all_gather.11 = bf16[8,64,512]{2,0,1:T(8,128)(2,1)S(1)} all-gather(bf16[8,8,512]{2,0,1:T(8,128)(2,1)S(1)} %copy.42), channel_id=1, replica_groups=mesh['groups'=2,'owner'=8,'tp'=2] {'owner'}, dimensions={1}, use_global_device_ids=true | all-gather | bytes 589824 | tf_op jit(solution)/shard_map/all_gather | solution.py:42
  164.6 0.3 convolution_convert_fusion
  164.9 0.2 copy.46
  165.2 1.9 copy-done.1
  167.1 1.6 convolution_bitcast_fusion
  168.7 12.7 %all-reduce.2 = bf16[512,64]{0,1:T(8,128)(2,1)S(1)} all-reduce(f32[512,64]{0,1:T(8,128)S(1)} %bitcast.42), channel_id=1, replica_groups=mesh['groups'=2,'owner'=8,'tp'=2] {'tp'}, use_global_device_ids=true, to_apply=%region_2.3 | all-reduce | flops 32768 | bytes 196608 | tf_op jit(solution)/shard_map/psum | solution.py:60
  181.5 0.3 fusion.7
  181.8 0.7 reduce-scatter.2.cloned.1.call-done
  182.5 2.2 %fusion.15 = (bf16[512,512]{1,0:T(8,128)(2,1)}, f32[512,512]{1,0:T(8,128)S(1)}) fusion(f32[512,512]{1,0:T(8,128)} %reduce-scatter.2.cloned.1.call-done, f32[4,128,512]{2,1,0:T(8,128)S(1)} %fusion.7), kind=kLoop, calls=%fused_computation.32 | loop fusion | flops 524288 | bytes 3670016 | tf_op jit(solution)/shard_map/convert_element_type | solution.py:64
  184.7 1.2 fusion
  185.9 0.2 select_reduce_fusion.2
  186.1 4.9 %psum.15 = f32[4]{0:T(128)S(1)} all-reduce(f32[4]{0:T(128)S(1)} %select_reduce_fusion.2), channel_id=1, replica_groups=mesh['groups'=2,'owner'=8,'tp'=2] {'tp'}, use_global_device_ids=true, to_apply=%region_5.6 | all-reduce | flops 4 | bytes 32 | tf_op jit(solution)/shard_map/psum | solution.py:70
  191.0 0.1 select_reduce_fusion.1
  191.1 15.4 %pmax.7 = f32[16]{0:T(128)S(1)} all-reduce(f32[16]{0:T(128)S(1)} %select_reduce_fusion.1), channel_id=1, replica_groups=mesh['groups'=2,'owner'=8,'tp'=2] {'owner'}, use_global_device_ids=true, to_apply=%region_7.8 | all-reduce | flops 16 | bytes 128 | tf_op jit(solution)/shard_map/pmax | solution.py:85
  206.5 0.6 dynamic_slice.3
  (20 shorter events, 0.1 us)
Async XLA Ops:
  7.2 14.5 %copy-start = (bf16[8,512,64]{1,2,0:T(8,128)(2,1)S(1)}, bf16[8,512,64]{1,2,0:T(8,128)(2,1)}, u32[]{:S(2)}) copy-start(bf16[8,512,64]{1,2,0:T(8,128)(2,1)} %param.12) | copy-start | bytes 1572868
  7.2 131.7 %all-gather.2.cloned.1.call-start = ((), (), s32[]{:S(2)}) async-start(), calls=%async_computation.2 | async-start | bytes 9437184 | tf_op jit(solution)/shard_map/all_gather | solution.py:56
  23.8 141.1 %all-to-all-start = ((bf16[4,8,512,64]{2,3,0,1:T(8,128)(2,1)}), bf16[4,8,512,64]{2,3,0,1:T(8,128)(2,1)S(1)}, u32[]{:S(2)}, u32[]{:S(2)}) async-start(bf16[4,8,512,64]{2,3,0,1:T(8,128)(2,1)} %copy.39), calls=%async_computation.1 | async-start | bytes 4194304 | tf_op jit(solution)/shard_map/all_to_all | solution.py:41
  27.4 122.0 %copy-start.2 = (bf16[8,8,512]{2,1,0:T(8,128)(2,1)S(1)}, bf16[8,8,512]{2,1,0:T(8,128)(2,1)}, u32[]{:S(2)}) copy-start(bf16[8,8,512]{2,1,0:T(8,128)(2,1)} %param.13) | copy-start | bytes 196612
  27.4 122.1 %copy-start.5 = (s32[16]{0:T(128)S(1)}, s32[16]{0:T(128)}, u32[]{:S(2)}) copy-start(s32[16]{0:T(128)} %param.19) | copy-start | bytes 196
  27.5 122.1 %copy-start.6 = (s32[4]{0:T(128)S(1)}, s32[4]{0:T(128)}, u32[]{:S(2)}) copy-start(s32[4]{0:T(128)} %param.18) | copy-start | bytes 52
  27.5 155.0 %reduce-scatter.2.cloned.1.call-start = ((), (), s32[]{:S(2)}) async-start(), calls=%async_computation.3 | async-start | bytes 3145728 | tf_op jit(solution)/shard_map/reduce_scatter | solution.py:59
  164.9 2.2 %copy-start.1 = (bf16[512,4096]{1,0:T(8,128)(2,1)S(1)}, bf16[512,4096]{1,0:T(8,128)(2,1)}, u32[]{:S(2)}) copy-start(bf16[512,4096]{1,0:T(8,128)(2,1)} %param.10) | copy-start | bytes 12582916
  168.7 16.0 %copy-start.4 = (f32[512]{0:T(512)S(1)}, f32[512]{0:T(512)}, u32[]{:S(2)}) copy-start(f32[512]{0:T(512)} %param.14) | copy-start | bytes 6148
  181.8 4.1 %copy-start.3 = (s32[4]{0:T(128)S(1)}, s32[4]{0:T(128)}, u32[]{:S(2)}) copy-start(s32[4]{0:T(128)} %param.17) | copy-start | bytes 52
Sparse Core Ops, SparseCore 0:
  9.6 129.2 all-gather.1
  149.6 32.8 reduce-scatter.1
where the time goes:
time: 214 us
  waiting for transfers between devices  113 us (53%)
  blocking collectives  58.5 us (27%)
  between operations  14.9 us (7%)
  matrix products  14 us (7%)
  local copies, waits for them, and re-layouts  6.68 us (3%)
  starting transfers between devices  3.68 us (2%)
  other arithmetic  3.44 us (2%)
    all_gather x1, waiting for transfers between devices, shards(): lax.all_gather(base_value_weight, 'owner', axis=0, tiled=True)  111 us
    pmax x1, blocking collectives, shards(): merged = lax.pmax(candidate, 'owner')  15.4 us
    all_gather x1, blocking collectives, shards(): lax.all_gather(adapter_up_factor, 'owner', axis=1, tiled=True)  14.8 us
    psum x1, blocking collectives, shards(): low_rank = lax.psum(low_part, 'tp').astype(jnp.bfloat16)  12.7 us
    unnamed x1, blocking collectives  10.6 us
    dot_general x1, matrix products, shards(): jnp.dot(tokens, lax.all_gather(base_value_weight, 'owner', axis=0, tiled=...  10.5 us
    psum x1, blocking collectives, shards(): lax.psum(passage_part, 'tp')  4.94 us
  transfers between devices with their start and end apart: 3, of which 2 were waited for; matrix products, arithmetic and copies ran while one was open for 8% of the time, Pallas kernels for 0%

commit v1 on v0

v1 whole, which is shorter than its diff:
```python
import functools

import jax
import jax.numpy as jnp
from jax import lax
from jax.experimental import pallas as pl
from jax.experimental.pallas import tpu as pltpu
from jax.sharding import PartitionSpec as P

TILE = 128
CORES = 2
LOWEST = -1e30
MESH = pl.DeviceIdType.MESH
F32 = jnp.float32
BF16 = jnp.bfloat16


class Plan:
    def __init__(self, n_owner, n_tp, tokens, weight, down, up, docs):
        self.n_owner, self.n_tp = n_owner, n_tp
        self.nz = n_owner // CORES
        self.tok, self.feat = tokens.shape
        self.tiles = self.tok // TILE
        self.rows = weight.shape[0]
        self.cols = weight.shape[1] // n_tp
        self.adapters, _, self.rank = down.shape
        self.wide = self.adapters * self.rank
        self.rank_rows = up.shape[1]
        self.up_rows = self.adapters * self.rank_rows
        self.docs = docs
        self.doc_dev = docs // n_owner
        self.lanes = -(-docs // 128) * 128
        self.flat = self.rows % 128 == 0
        self.parts_w = 2 if self.rows >= 256 else 1
        self.groups = list(range(n_tp - 1)) + ["d", n_tp - 1]
        self.part_of, self.parts = {}, 0
        for g in self.groups:
            count = 2 if g == "d" else self.parts_w
            self.part_of[g] = list(range(self.parts, self.parts + count))
            self.parts += count


def kernel(
    p,
    tok_hbm, w_hbm, d_hbm, u_hbm, rel_ref, tile_adapter, storage, live, passage_doc, doc_slot,
    out_hbm, score_ref,
    tok, wbuf, dbuf, ubuf, acc, low, low_in, sums_in, term, out, marks,
    load_sem, z_recv, y_recv, c_recv, up_send, down_send, y_send, c_send,
    x_send, x_recv, l_send, l_recv, m_send, m_recv, out_sem,
):
    gi, owner, tp = lax.axis_index("groups"), lax.axis_index("owner"), lax.axis_index("tp")
    zi, ci = owner // CORES, owner % CORES
    devices = p.n_tp * p.n_owner
    me = tp * p.n_owner + owner

    barrier = pltpu.get_barrier_semaphore()

    def greet(k, carry):
        peer = lax.rem(me + k, devices)
        pl.semaphore_signal(
            barrier, inc=1, device_id={"tp": peer // p.n_owner, "owner": lax.rem(peer, p.n_owner)},
            device_id_type=MESH,
        )
        return carry

    lax.fori_loop(1, devices, greet, 0)
    pl.semaphore_signal(barrier, inc=1, device_id={"groups": 1 - gi}, device_id_type=MESH)

    def columns(g):
        t = lax.rem(tp + 1 + g, p.n_tp)
        return pl.ds(pl.multiple_of(t * p.cols, 128), p.cols)

    own_rows = pl.ds(pl.multiple_of(owner * p.rows, p.rows), p.rows)
    loads = []
    for g in p.groups:
        if g == "d":
            there = dbuf.at[owner] if p.flat else dbuf.at[own_rows]
            loads.append((d_hbm, there))
            loads.append((u_hbm, ubuf.at[pl.ds(pl.multiple_of(owner * p.up_rows, p.up_rows), p.up_rows)]))
        else:
            loads.append((w_hbm.at[:, columns(g)], wbuf.at[g, own_rows]))
    loads.append((tok_hbm, tok))
    loads = [pltpu.make_async_copy(a, b, load_sem.at[i]) for i, (a, b) in enumerate(loads)]
    for load in loads:
        load.start()
    for load in loads[:-1]:
        load.wait()
    pl.semaphore_wait(barrier, devices)

    def piece(part, z, c, h):
        o = z * CORES + c
        for g in p.groups:
            if part in p.part_of[g]:
                k = p.part_of[g].index(part)
                break
        if g == "d":
            if k == 1:
                half = p.up_rows // 2
                return ubuf.at[pl.ds(pl.multiple_of(o * p.up_rows + h * half, half), half)]
            if p.flat:
                half = p.wide // 2
                return dbuf.at[o, pl.ds(pl.multiple_of(h * half, half), half)]
            half = p.rows // 2
            return dbuf.at[pl.ds(pl.multiple_of(o * p.rows + h * half, half), half)]
        half = p.rows // 2
        size = half // p.parts_w
        return wbuf.at[g, pl.ds(pl.multiple_of(o * p.rows + h * half + k * size, size), size)]

    def send(part, z, c, h, send_sem, recv_sem, device):
        ref = piece(part, z, c, h)
        return pltpu.make_async_remote_copy(
            src_ref=ref, dst_ref=ref, send_sem=send_sem, recv_sem=recv_sem,
            device_id=device, device_id_type=MESH,
        )

    def up(part, z):
        return send(part, z, ci, gi, up_send.at[part, z], z_recv.at[part, z],
                    {"owner": lax.rem(owner + CORES, p.n_owner)})

    def down(part, z):
        return send(part, z, ci, gi, down_send.at[part, z], z_recv.at[part, z],
                    {"owner": lax.rem(owner + p.n_owner - CORES, p.n_owner)})

    def across(part, z, h=None):
        return send(part, z, ci, gi if h is None else h, y_send.at[part, z], y_recv.at[part, z],
                    {"groups": 1 - gi})

    def beside(part, z, c, h):
        return send(part, z, c, h, c_send.at[part, z, h], c_recv.at[part, z, h],
                    {"owner": zi * CORES + 1 - ci})

    def own_sends(g):
        for part in p.part_of[g]:
            @pl.when(zi + 1 < p.nz)
            def _():
                up(part, zi).start()

            @pl.when(zi > 0)
            def _():
                down(part, zi).start()
            for h in range(2):
                beside(part, zi, ci, h).start()

    def each_way(s, body):
        @pl.when(zi - s >= 0)
        def _():
            body(zi - s, True)

        @pl.when(zi + s < p.nz)
        def _():
            body(zi + s, False)

    def stage_z(g, s):
        def body(z, upward):
            for part in p.part_of[g]:
                up(part, z).wait_recv()
                if upward:
                    @pl.when(zi + 1 < p.nz)
                    def _():
                        up(part, z).start()
                else:
                    @pl.when(zi > 0)
                    def _():
                        down(part, z).start()
                across(part, z).start()
                beside(part, z, ci, gi).start()
        each_way(s, body)

    def stage_y(g, s):
        def body(z, upward):
            for part in p.part_of[g]:
                across(part, z, 1 - gi).wait_recv()
                beside(part, z, ci, 1 - gi).start()
        each_way(s, body)

    def slot_of(g):
        return p.n_tp if g == "d" else g

    def add_block(g, z, first):
        span = CORES * p.rows
        rows = TILE

        def body(j, carry):
            r = pl.ds(pl.multiple_of(j * rows, rows), rows)
            if g == "d":
                total = None
                for c in range(CORES):
                    f = pl.ds(pl.multiple_of(z * span + c * p.rows, 128), p.rows)
                    part = lax.dot_general(tok[r, f], dbuf[z * CORES + c], (((1,), (1,)), ((), ())),
                                           preferred_element_type=F32)
                    total = part if total is None else total + part
                low[r] = total if first else low[r] + total
            else:
                f = pl.ds(pl.multiple_of(z * span, 128), span)
                k = pl.ds(pl.multiple_of(z * span, span), span)
                part = jnp.dot(tok[r, f], wbuf[g, k], preferred_element_type=F32)
                acc[g, r] = part if first else acc[g, r] + part
            return carry

        lax.fori_loop(0, p.tiles, body, 0)

    def all_blocks(g):
        def body(j, carry):
            r = pl.ds(pl.multiple_of(j * TILE, TILE), TILE)
            if g == "d":
                low[r] = jnp.dot(tok[r], dbuf[...], preferred_element_type=F32)
            else:
                acc[g, r] = jnp.dot(tok[r], wbuf[g], preferred_element_type=F32)
            return carry

        lax.fori_loop(0, p.tiles, body, 0)

    def stage_c(g, s):
        def body(z, upward):
            for part in p.part_of[g]:
                for h in range(2):
                    beside(part, z, 1 - ci, h).wait_recv()
            if p.flat:
                add_block(g, z, s == 0)
        if s == 0:
            body(zi, True)
        else:
            each_way(s, body)

    def to_tp(ref_src, ref_dst, k, s_sem, r_sem):
        return pltpu.make_async_remote_copy(
            src_ref=ref_src, dst_ref=ref_dst, send_sem=s_sem.at[k], recv_sem=r_sem.at[k],
            device_id={"tp": lax.rem(tp + 1 + k, p.n_tp)}, device_id_type=MESH,
        )

    def sums_copy(k):
        return to_tp(acc.at[k], sums_in.at[k], k, x_send, x_recv)

    def low_copy(k):
        return to_tp(low_in.at[p.n_tp - 1], low_in.at[k], k, l_send, l_recv)

    def slot_at(j):
        return storage[tile_adapter[j]]

    def pick_low():
        def body(j, carry):
            r = pl.ds(pl.multiple_of(j * TILE, TILE), TILE)
            slot = slot_at(j)
            lane = lax.broadcasted_iota(jnp.int32, (TILE, 128), 1)
            total = jnp.zeros((TILE, 128), F32)
            for pair in range(p.wide // 128):
                here = (pair * 128 + lane) // p.rank == slot
                total = total + jnp.where(here, low[r, pair * 128:(pair + 1) * 128], 0.0)
            low_in[p.n_tp - 1, r] = total
            return carry

        lax.fori_loop(0, p.tiles, body, 0)

    def finish(g):
        if not p.flat:
            all_blocks(g)
        if g == "d":
            pick_low()
            for k in range(p.n_tp - 1):
                low_copy(k).start()
        elif g < p.n_tp - 1:
            sums_copy(g).start()

    def adapter_term():
        for k in range(p.n_tp - 1):
            low_copy(k).wait_recv()
        row = lax.broadcasted_iota(jnp.int32, (128, p.wide), 0) % p.rank
        col = lax.broadcasted_iota(jnp.int32, (128, p.wide), 1)
        rank_of = (col // p.up_rows) * p.rank_rows + col % p.rank_rows
        spread = jnp.where(row == rank_of, 1.0, 0.0).astype(BF16)

        def body(j, carry):
            r = pl.ds(pl.multiple_of(j * TILE, TILE), TILE)
            slot = slot_at(j)
            total = low_in[p.n_tp - 1, r]
            for k in range(p.n_tp - 1):
                total = total + low_in[k, r]
            laid = jnp.dot(total.astype(BF16), spread, preferred_element_type=F32)
            lane = lax.broadcasted_iota(jnp.int32, (TILE, p.wide), 1)
            here = (lane // p.rank_rows) % p.adapters == slot
            laid = jnp.where(here, laid, 0.0).astype(BF16)
            term[r] = jnp.dot(laid, ubuf[...], preferred_element_type=F32)
            return carry

        lax.fori_loop(0, p.tiles, body, 0)

    steps = [(g, s) for g in p.groups for s in range(p.nz)]
    own_sends(p.groups[0])
    loads[-1].wait()
    for i in range(len(steps) + 2):
        if i < len(steps):
            g, s = steps[i]
            if s == 0:
                after = p.groups.index(g) + 1
                if after < len(p.groups):
                    own_sends(p.groups[after])
            else:
                stage_z(g, s)
        if 1 <= i <= len(steps):
            g, s = steps[i - 1]
            if s > 0:
                stage_y(g, s)
        if i == len(steps) - 1:
            c_before = steps[i - 2]
            stage_c(*c_before)
            if c_before[1] == p.nz - 1:
                finish(c_before[0])
            adapter_term()
        elif i >= 2:
            g, s = steps[i - 2]
            stage_c(g, s)
            if s == p.nz - 1:
                finish(g)

    for k in range(p.n_tp - 1):
        sums_copy(k).wait_recv()
    marks[me] = jnp.full((marks.shape[1], p.lanes), jnp.where(tp == 0, LOWEST, 0.0), F32)
    weight = rel_ref[...]

    def tile_out(j):
        r = pl.ds(pl.multiple_of(j * TILE, TILE), TILE)
        return pltpu.make_async_copy(out.at[r], out_hbm.at[r], out_sem.at[j])

    def last(j, carry):
        r = pl.ds(pl.multiple_of(j * TILE, TILE), TILE)
        adapted = acc[p.n_tp - 1, r]
        for k in range(p.n_tp - 1):
            adapted = adapted + sums_in[k, r]
        adapted = adapted + term[r]
        out[r] = adapted.astype(BF16)
        tile_out(j).start()
        scored = adapted / (1.0 + jnp.exp(-adapted)) * weight
        length = live[j]
        token = lax.broadcasted_iota(jnp.int32, scored.shape, 0)
        scored = jnp.where(token < length, scored, 0.0)
        part = jnp.sum(jnp.sum(scored, axis=0, keepdims=True), axis=1, keepdims=True)
        scale = jnp.sqrt(jnp.full((1, p.lanes), length, jnp.int32).astype(F32))
        slot = doc_slot[passage_doc[j]]
        lane = lax.broadcasted_iota(jnp.int32, (1, p.lanes), 1)
        empty = jnp.where(tp == 0, LOWEST, 0.0)
        marks[me, pl.ds(j, 1)] = jnp.where(lane == slot, part / scale, empty)
        return carry

    lax.fori_loop(0, p.tiles, last, 0)

    def mark_copy(k, slot, sender):
        peer = lax.rem(me + k, devices)
        return pltpu.make_async_remote_copy(
            src_ref=marks.at[slot], dst_ref=marks.at[slot], send_sem=m_send.at[k], recv_sem=m_recv.at[sender],
            device_id={"tp": peer // p.n_owner, "owner": lax.rem(peer, p.n_owner)}, device_id_type=MESH,
        )

    def mark_start(k, carry):
        mark_copy(k, me, me).start()
        return carry

    def mark_wait(k, carry):
        sender = lax.rem(me + k, devices)
        mark_copy(k, sender, sender).wait_recv()
        return carry

    def mark_sent(k, carry):
        mark_copy(k, me, me).wait_send()
        return carry

    lax.fori_loop(1, devices, mark_start, 0)

    for g in p.groups:
        for part in p.part_of[g]:
            for s in range(p.nz):
                def gone(z, upward):
                    if upward:
                        @pl.when(zi + 1 < p.nz)
                        def _():
                            up(part, z).wait_send()
                    if s == 0 or not upward:
                        @pl.when(zi > 0)
                        def _():
                            down(part, z).wait_send()
                    if s > 0:
                        across(part, z).wait_send()
                    for h in range(2):
                        beside(part, z, ci, h).wait_send()
                if s == 0:
                    gone(zi, True)
                else:
                    each_way(s, gone)
    for k in range(p.n_tp - 1):
        sums_copy(k).wait_send()
        low_copy(k).wait_send()

    lax.fori_loop(1, devices, mark_wait, 0)
    best = None
    for o in range(p.n_owner):
        total = marks[o]
        for t in range(1, p.n_tp):
            total = total + marks[t * p.n_owner + o]
        best = total if best is None else jnp.maximum(best, total)
    lane = lax.broadcasted_iota(jnp.int32, best.shape, 1)
    for d in range(p.doc_dev):
        score_ref[d] = jnp.max(jnp.where(lane == owner * p.doc_dev + d, best, 2 * LOWEST))

    lax.fori_loop(1, devices, mark_sent, 0)

    def out_wait(j, carry):
        tile_out(j).wait()
        return carry

    lax.fori_loop(0, p.tiles, out_wait, 0)


def shards(
    n_owner, n_tp,
    tokens,
    base_value_weight,
    adapter_down_factor,
    adapter_up_factor,
    relevance_weight,
    tile_adapter_index,
    adapter_storage_slot,
    tile_live_length,
    passage_document,
    document_output_slot,
):
    p = Plan(
        n_owner, n_tp, tokens, base_value_weight, adapter_down_factor, adapter_up_factor,
        document_output_slot.shape[0],
    )
    if p.flat:
        down = jnp.transpose(adapter_down_factor, (0, 2, 1)).reshape(p.wide, p.rows)
        dshape = (p.n_owner, p.wide, p.rows)
    else:
        down = jnp.transpose(adapter_down_factor, (1, 0, 2)).reshape(p.rows, p.wide)
        dshape = (p.feat, p.wide)
    up = adapter_up_factor.reshape(p.up_rows, p.cols)
    peers = max(1, p.n_tp - 1)
    devices = p.n_tp * p.n_owner
    dma = pltpu.SemaphoreType.DMA
    mark_rows = -(-p.tiles // 8) * 8
    hbm, smem = pl.BlockSpec(memory_space=pl.ANY), pl.BlockSpec(memory_space=pltpu.SMEM)
    return pl.pallas_call(
        functools.partial(kernel, p),
        out_shape=(
            jax.ShapeDtypeStruct((p.tok, p.cols), BF16),
            jax.ShapeDtypeStruct((p.doc_dev,), F32),
        ),
        in_specs=[hbm] * 4 + [pl.BlockSpec(memory_space=pltpu.VMEM)] + [smem] * 5,
        out_specs=(hbm, smem),
        scratch_shapes=[
            pltpu.VMEM((p.tok, p.feat), BF16),
            pltpu.VMEM((p.n_tp, p.feat, p.cols), BF16),
            pltpu.VMEM(dshape, BF16),
            pltpu.VMEM((p.wide, p.cols), BF16),
            pltpu.VMEM((p.n_tp, p.tok, p.cols), F32),
            pltpu.VMEM((p.tok, p.wide), F32),
            pltpu.VMEM((p.n_tp, p.tok, 128), F32),
            pltpu.VMEM((peers, p.tok, p.cols), F32),
            pltpu.VMEM((p.tok, p.cols), F32),
            pltpu.VMEM((p.tok, p.cols), BF16),
            pltpu.VMEM((devices, mark_rows, p.lanes), F32),
            dma((p.n_tp + 3,)),
            dma((p.parts, p.nz)),
            dma((p.parts, p.nz)),
            dma((p.parts, p.nz, 2)),
            dma((p.parts, p.nz)),
            dma((p.parts, p.nz)),
            dma((p.parts, p.nz)),
            dma((p.parts, p.nz, 2)),
            dma((peers,)),
            dma((peers,)),
            dma((peers,)),
            dma((peers,)),
            dma((devices,)),
            dma((devices,)),
            dma((p.tiles,)),
        ],
        compiler_params=pltpu.CompilerParams(
            collective_id=0, has_side_effects=True, vmem_limit_bytes=60 * 1024 * 1024
        ),
        name="gather_project_score",
    )(
        tokens, base_value_weight, down, up, relevance_weight.reshape(1, p.cols),
        tile_adapter_index, adapter_storage_slot, tile_live_length, passage_document, document_output_slot,
    )


def solution(mesh):
    placed = (
        P(("groups", "owner"), "tp"),
        P(("tp", "owner"), None),
        P(None, ("tp", "owner"), None),
        P(None, "owner", "tp"),
        P("tp"),
        P(("groups", "owner")),
        P(),
        P(("groups", "owner")),
        P(("groups", "owner")),
        P("groups"),
    )
    return jax.shard_map(
        functools.partial(shards, mesh.shape["owner"], mesh.shape["tp"]),
        mesh=mesh,
        in_specs=placed,
        out_specs=(P(("groups", "owner"), "tp"), P(("groups", "owner"))),
        check_vma=False,
    )
```

time: 214 us -> 94.1 us (0.44)
  waiting for transfers between devices: 113 us -> 0 us
  Pallas kernels: 0 us -> 90.3 us
  blocking collectives: 58.5 us -> 0 us
  between operations: 14.9 us -> 0.64 us
  matrix products: 14 us -> 0 us
  local copies, waits for them, and re-layouts: 6.68 us -> 2.97 us
  starting transfers between devices: 3.68 us -> 0 us
  other arithmetic: 3.44 us -> 0 us
    all_gather x1 -> x0, waiting for transfers between devices: 111 us -> none  [shards(): lax.all_gather(base_value_weight, 'owner', axis=0, tiled=True)]
    pallas_call x0 -> x1, Pallas kernels: none -> 90.3 us  [shards(): pl.pallas_call(functools.partial(kernel, p), out_shape=(jax.ShapeDtypeStr...]
    psum x2 -> x0, blocking collectives: 17.7 us -> none  [the longest x1 12.7 us: shards(): low_rank = lax.psum(low_part, 'tp').astype(jnp.bfloat16)]
    pmax x1 -> x0, blocking collectives: 15.4 us -> none  [shards(): merged = lax.pmax(candidate, 'owner')]
    all_gather x1 -> x0, blocking collectives: 14.8 us -> none  [shards(): lax.all_gather(adapter_up_factor, 'owner', axis=1, tiled=True)]
    dot_general x5 -> x0, matrix products: 14 us -> none  [the longest x1 10.5 us: shards(): jnp.dot(tokens, lax.all_gather(base_value_weight, 'owner', axis=0, tiled=...]
    unnamed x1 -> x0, blocking collectives: 10.6 us -> none
    all_to_all x1 -> x0, starting transfers between devices: 3.6 us -> none  [shards(): lax.all_to_all(down_projected, 'owner', split_axis=1, concat_axis=1, tile...]
  transfers between devices with their start and end apart: 3 -> 0, of which waited for: 2 -> 0; matrix products, arithmetic and copies ran while one was open for 8% -> 0% of each run, Pallas kernels for 0% -> 0%
where the time goes in v1:
time: 94.1 us; the launch traced here: 93.9 us
  Pallas kernels  90.3 us (96%)
  local copies, waits for them, and re-layouts  2.97 us (3%)
    pallas_call x1, Pallas kernels, shards(): pl.pallas_call(functools.partial(kernel, p), out_shape=(jax.ShapeDtypeStr...  90.3 us
    unnamed x2, local copies, waits for them, and re-layouts  2.97 us

profile of v1, /device:TPU:0, one launch (start us, length us, event | category | flops | bytes accessed | tf_op | source)
XLA Modules:
  0.0 93.9 jit_solution(18315534248691906531)
XLA Ops:
  0.6 90.3 %gather_project_score.1 = (bf16[512,512]{1,0:T(8,128)(2,1)}, f32[2]{0:T(128)}) custom-call(bf16[512,4096]{1,0:T(8,128)(2,1)} %tok_hbm.1, bf16[512,1024]{1,0:T(8,128)(2,1)} %w_hbm.1, bf16[512,512]{1,0:T(8,128)(2,1)} %bitcast.5, bf16[64,512]{1,0:T(8,128)(2,1)} %bitcast.6, f32[1,512]{1,0:T(1,128)} %bitcast.7, s32[4]{0:T(128)} %tile_adapter.1, s32[8]{0:T(128)} %storage.1, ...), custom_call_target="tpu_custom_call" | custom-call | tf_op jit(solution)/shard_map/gather_project_score/pallas_call | solution.py:441
  91.0 1.9 %copy.14 = bf16[512,512]{1,0:T(8,128)(2,1)} copy(bf16[512,512]{1,0:T(8,128)(2,1)} %get-tuple-element.4) | data formatting | bytes 1048576
  92.8 1.1 %copy.15 = f32[2]{0:T(128)} copy(f32[2]{0:T(128)} %get-tuple-element.5) | data formatting | bytes 16

commit v2 on v1

--- a/solution.py
+++ b/solution.py
@@ -10,6 +10,7 @@
 TILE = 128
 CORES = 2
 LOWEST = -1e30
+LAGS = (1, 2)
 MESH = pl.DeviceIdType.MESH
 F32 = jnp.float32
 BF16 = jnp.bfloat16
@@ -31,11 +32,13 @@
         self.doc_dev = docs // n_owner
         self.lanes = -(-docs // 128) * 128
         self.flat = self.rows % 128 == 0
-        self.parts_w = 2 if self.rows >= 256 else 1
+        self.parts_w = {g: (4 if g == n_tp - 1 else 2) if self.rows >= 256 else 1 for g in range(n_tp)}
+        self.parts_d = 2 if self.flat else 1
+        self.whole = self.nz >= 4
         self.groups = list(range(n_tp - 1)) + ["d", n_tp - 1]
         self.part_of, self.parts = {}, 0
         for g in self.groups:
-            count = 2 if g == "d" else self.parts_w
+            count = self.parts_d + 1 if g == "d" else self.parts_w[g]
             self.part_of[g] = list(range(self.parts, self.parts + count))
             self.parts += count
 
@@ -45,7 +48,7 @@
     tok_hbm, w_hbm, d_hbm, u_hbm, rel_ref, tile_adapter, storage, live, passage_doc, doc_slot,
     out_hbm, score_ref,
     tok, wbuf, dbuf, ubuf, acc, low, low_in, sums_in, term, out, marks,
-    load_sem, z_recv, y_recv, c_recv, up_send, down_send, y_send, c_send,
+    load_sem, z_recv, y_recv, c_recv, e_recv, up_send, down_send, y_send, c_send, e_send,
     x_send, x_recv, l_send, l_recv, m_send, m_recv, out_sem,
 ):
     gi, owner, tp = lax.axis_index("groups"), lax.axis_index("owner"), lax.axis_index("tp")
@@ -55,24 +58,31 @@
 
     barrier = pltpu.get_barrier_semaphore()
 
-    def greet(k, carry):
-        peer = lax.rem(me + k, devices)
-        pl.semaphore_signal(
-            barrier, inc=1, device_id={"tp": peer // p.n_owner, "owner": lax.rem(peer, p.n_owner)},
-            device_id_type=MESH,
-        )
-        return carry
-
-    lax.fori_loop(1, devices, greet, 0)
-    pl.semaphore_signal(barrier, inc=1, device_id={"groups": 1 - gi}, device_id_type=MESH)
+    def greet(**device):
+        pl.semaphore_signal(barrier, inc=1, device_id=device, device_id_type=MESH)
+
+    @pl.when(zi + 1 < p.nz)
+    def _():
+        greet(owner=lax.rem(owner + CORES, p.n_owner))
+
+    @pl.when(zi > 0)
+    def _():
+        greet(owner=lax.rem(owner + p.n_owner - CORES, p.n_owner))
+
+    greet(groups=1 - gi)
+    greet(owner=zi * CORES + 1 - ci)
+    for k in range(p.n_tp - 1):
+        greet(tp=lax.rem(tp + 1 + k, p.n_tp))
+    met = p.n_tp + 1 + jnp.where(zi > 0, 1, 0) + jnp.where(zi + 1 < p.nz, 1, 0)
 
     def columns(g):
         t = lax.rem(tp + 1 + g, p.n_tp)
         return pl.ds(pl.multiple_of(t * p.cols, 128), p.cols)
 
     own_rows = pl.ds(pl.multiple_of(owner * p.rows, p.rows), p.rows)
-    loads = []
+    loads, loads_of = [], {}
     for g in p.groups:
+        loads_of[g] = [len(loads)] + ([len(loads) + 1] if g == "d" else [])
         if g == "d":
             there = dbuf.at[owner] if p.flat else dbuf.at[own_rows]
             loads.append((d_hbm, there))
@@ -83,9 +93,7 @@
     loads = [pltpu.make_async_copy(a, b, load_sem.at[i]) for i, (a, b) in enumerate(loads)]
     for load in loads:
         load.start()
-    for load in loads[:-1]:
-        load.wait()
-    pl.semaphore_wait(barrier, devices)
+    pl.semaphore_wait(barrier, met)
 
     def piece(part, z, c, h):
         o = z * CORES + c
@@ -94,16 +102,17 @@
                 k = p.part_of[g].index(part)
                 break
         if g == "d":
-            if k == 1:
+            if k == p.parts_d:
                 half = p.up_rows // 2
                 return ubuf.at[pl.ds(pl.multiple_of(o * p.up_rows + h * half, half), half)]
             if p.flat:
                 half = p.wide // 2
-                return dbuf.at[o, pl.ds(pl.multiple_of(h * half, half), half)]
+                size = half // p.parts_d
+                return dbuf.at[o, pl.ds(pl.multiple_of(h * half + k * size, size), size)]
             half = p.rows // 2
             return dbuf.at[pl.ds(pl.multiple_of(o * p.rows + h * half, half), half)]
         half = p.rows // 2
-        size = half // p.parts_w
+        size = half // p.parts_w[g]
         return wbuf.at[g, pl.ds(pl.multiple_of(o * p.rows + h * half + k * size, size), size)]
 
     def send(part, z, c, h, send_sem, recv_sem, device):
@@ -129,7 +138,17 @@
         return send(part, z, c, h, c_send.at[part, z, h], c_recv.at[part, z, h],
                     {"owner": zi * CORES + 1 - ci})
 
+    def extra(part, i):
+        step = CORES if i == 0 else p.n_owner - CORES
+        return send(part, zi, ci, 1 - gi, e_send.at[part, i], e_recv.at[part, i],
+                    {"owner": lax.rem(owner + step, p.n_owner)})
+
+    def extra_in(part, z, i):
+        return send(part, z, ci, 1 - gi, e_send.at[part, i], e_recv.at[part, i], {"groups": 1 - gi})
+
     def own_sends(g):
+        for i in loads_of[g]:
+            loads[i].wait()
         for part in p.part_of[g]:
             @pl.when(zi + 1 < p.nz)
             def _():
@@ -140,6 +159,12 @@
                 down(part, zi).start()
             for h in range(2):
                 beside(part, zi, ci, h).start()
+        if p.whole:
+            for i, edge in enumerate((0, p.nz - 1)):
+                @pl.when(zi == edge)
+                def _():
+                    for part in p.part_of[g]:
+                        extra(part, i).start()
 
     def each_way(s, body):
         @pl.when(zi - s >= 0)
@@ -149,6 +174,20 @@
         @pl.when(zi + s < p.nz)
         def _():
             body(zi + s, False)
+
+    def via_twin(s, upward, body, other=None):
+        if not (p.whole and s == 1):
+            body()
+            return
+        straight = zi == (1 if upward else p.nz - 2)
+
+        @pl.when(jnp.logical_not(straight))
+        def _():
+            body()
+        if other is not None:
+            @pl.when(straight)
+            def _():
+                other()
 
     def stage_z(g, s):
         def body(z, upward):
@@ -162,14 +201,15 @@
                     @pl.when(zi > 0)
                     def _():
                         down(part, z).start()
-                across(part, z).start()
+                via_twin(s, upward, across(part, z).start)
                 beside(part, z, ci, gi).start()
         each_way(s, body)
 
     def stage_y(g, s):
         def body(z, upward):
             for part in p.part_of[g]:
-                across(part, z, 1 - gi).wait_recv()
+                via_twin(s, upward, lambda: across(part, z, 1 - gi).wait_recv(),
+                         lambda: extra_in(part, z, 0 if upward else 1).wait_recv())
                 beside(part, z, ci, 1 - gi).start()
         each_way(s, body)
 
@@ -263,6 +303,7 @@
 
     def adapter_term():
         for k in range(p.n_tp - 1):
+            sums_copy(k).wait_recv()
             low_copy(k).wait_recv()
         row = lax.broadcasted_iota(jnp.int32, (128, p.wide), 0) % p.rank
         col = lax.broadcasted_iota(jnp.int32, (128, p.wide), 1)
@@ -279,41 +320,48 @@
             lane = lax.broadcasted_iota(jnp.int32, (TILE, p.wide), 1)
             here = (lane // p.rank_rows) % p.adapters == slot
             laid = jnp.where(here, laid, 0.0).astype(BF16)
-            term[r] = jnp.dot(laid, ubuf[...], preferred_element_type=F32)
+            total = jnp.dot(laid, ubuf[...], preferred_element_type=F32)
+            for k in range(p.n_tp - 1):
+                total = total + sums_in[k, r]
+            term[r] = total
             return carry
 
         lax.fori_loop(0, p.tiles, body, 0)
 
     steps = [(g, s) for g in p.groups for s in range(p.nz)]
+    final = len(steps) - 1
+
+    def add_up(i):
+        g, s = steps[i]
+        stage_c(g, s)
+        if s == p.nz - 1:
+            finish(g)
+
+    ahead_y, ahead_c = LAGS
     own_sends(p.groups[0])
     loads[-1].wait()
-    for i in range(len(steps) + 2):
-        if i < len(steps):
-            g, s = steps[i]
-            if s == 0:
-                after = p.groups.index(g) + 1
-                if after < len(p.groups):
-                    own_sends(p.groups[after])
-            else:
-                stage_z(g, s)
-        if 1 <= i <= len(steps):
-            g, s = steps[i - 1]
-            if s > 0:
-                stage_y(g, s)
-        if i == len(steps) - 1:
-            c_before = steps[i - 2]
-            stage_c(*c_before)
-            if c_before[1] == p.nz - 1:
-                finish(c_before[0])
+    for i, (g, s) in enumerate(steps):
+        if i == final:
+            add_up(i - ahead_c)
             adapter_term()
-        elif i >= 2:
-            g, s = steps[i - 2]
-            stage_c(g, s)
-            if s == p.nz - 1:
-                finish(g)
-
-    for k in range(p.n_tp - 1):
-        sums_copy(k).wait_recv()
+        if s > 0:
+            stage_z(g, s)
+        if s == max(0, p.nz - 2):
+            after = p.groups.index(g) + 1
+            if after < len(p.groups):
+                own_sends(p.groups[after])
+        if i >= ahead_y and steps[i - ahead_y][1] > 0:
+            stage_y(*steps[i - ahead_y])
+        if ahead_c <= i < final:
+            add_up(i - ahead_c)
+    for i in range(final - ahead_y + 1, final):
+        if steps[i][1] > 0:
+            stage_y(*steps[i])
+    for i in range(final - ahead_c + 1, final):
+        add_up(i)
+    stage_y(*steps[final])
+    add_up(final)
+
     marks[me] = jnp.full((marks.shape[1], p.lanes), jnp.where(tp == 0, LOWEST, 0.0), F32)
     weight = rel_ref[...]
 
@@ -323,10 +371,7 @@
 
     def last(j, carry):
         r = pl.ds(pl.multiple_of(j * TILE, TILE), TILE)
-        adapted = acc[p.n_tp - 1, r]
-        for k in range(p.n_tp - 1):
-            adapted = adapted + sums_in[k, r]
-        adapted = adapted + term[r]
+        adapted = acc[p.n_tp - 1, r] + term[r]
         out[r] = adapted.astype(BF16)
         tile_out(j).start()
         scored = adapted / (1.0 + jnp.exp(-adapted)) * weight
@@ -378,13 +423,18 @@
                         def _():
                             down(part, z).wait_send()
                     if s > 0:
-                        across(part, z).wait_send()
+                        via_twin(s, upward, across(part, z).wait_send)
                     for h in range(2):
                         beside(part, z, ci, h).wait_send()
                 if s == 0:
                     gone(zi, True)
                 else:
                     each_way(s, gone)
+            if p.whole:
+                for i, edge in enumerate((0, p.nz - 1)):
+                    @pl.when(zi == edge)
+                    def _():
+                        extra(part, i).wait_send()
     for k in range(p.n_tp - 1):
         sums_copy(k).wait_send()
         low_copy(k).wait_send()
@@ -462,10 +512,12 @@
             dma((p.parts, p.nz)),
             dma((p.parts, p.nz)),
             dma((p.parts, p.nz, 2)),
+            dma((p.parts, 2)),
             dma((p.parts, p.nz)),
             dma((p.parts, p.nz)),
             dma((p.parts, p.nz)),
             dma((p.parts, p.nz, 2)),
+            dma((p.parts, 2)),
             dma((peers,)),
             dma((peers,)),
             dma((peers,)),

time: 94.1 us -> 85.3 us (0.906)
  Pallas kernels: 90.3 us -> 81.5 us
    pallas_call x1, Pallas kernels: 90.3 us -> 81.5 us  [shards(): pl.pallas_call(functools.partial(kernel, p), out_shape=(jax.ShapeDtypeStr...]
where the time goes in v2:
time: 85.3 us; the launch traced here: 85.1 us
  Pallas kernels  81.5 us (96%)
  local copies, waits for them, and re-layouts  2.97 us (3%)
    pallas_call x1, Pallas kernels, shards(): pl.pallas_call(functools.partial(kernel, p), out_shape=(jax.ShapeDtypeStr...  81.5 us
    unnamed x2, local copies, waits for them, and re-layouts  2.97 us

profile of v2, /device:TPU:0, one launch (start us, length us, event | category | flops | bytes accessed | tf_op | source)
XLA Modules:
  0.0 85.1 jit_solution(17234053761425451924)
XLA Ops:
  0.6 81.5 %gather_project_score.1 = (bf16[512,512]{1,0:T(8,128)(2,1)}, f32[2]{0:T(128)}) custom-call(bf16[512,4096]{1,0:T(8,128)(2,1)} %tok_hbm.1, bf16[512,1024]{1,0:T(8,128)(2,1)} %w_hbm.1, bf16[512,512]{1,0:T(8,128)(2,1)} %bitcast.5, bf16[64,512]{1,0:T(8,128)(2,1)} %bitcast.6, f32[1,512]{1,0:T(1,128)} %bitcast.7, s32[4]{0:T(128)} %tile_adapter.1, s32[8]{0:T(128)} %storage.1, ...), custom_call_target="tpu_custom_call" | custom-call | tf_op jit(solution)/shard_map/gather_project_score/pallas_call | solution.py:491
  82.2 1.9 %copy.14 = bf16[512,512]{1,0:T(8,128)(2,1)} copy(bf16[512,512]{1,0:T(8,128)(2,1)} %get-tuple-element.4) | data formatting | bytes 1048576
  84.0 1.1 %copy.15 = f32[2]{0:T(128)} copy(f32[2]{0:T(128)} %get-tuple-element.5) | data formatting | bytes 16

commit v3 on v2

--- a/solution.py
+++ b/solution.py
@@ -341,19 +341,18 @@
     own_sends(p.groups[0])
     loads[-1].wait()
     for i, (g, s) in enumerate(steps):
-        if i == final:
-            add_up(i - ahead_c)
-            adapter_term()
         if s > 0:
             stage_z(g, s)
         if s == max(0, p.nz - 2):
             after = p.groups.index(g) + 1
             if after < len(p.groups):
                 own_sends(p.groups[after])
+        if ahead_c <= i < final:
+            add_up(i - ahead_c)
         if i >= ahead_y and steps[i - ahead_y][1] > 0:
             stage_y(*steps[i - ahead_y])
-        if ahead_c <= i < final:
-            add_up(i - ahead_c)
+    add_up(final - ahead_c)
+    adapter_term()
     for i in range(final - ahead_y + 1, final):
         if steps[i][1] > 0:
             stage_y(*steps[i])

time: 85.3 us -> 83.4 us (0.978)
  Pallas kernels: 81.5 us -> 79.6 us
    pallas_call x1, Pallas kernels: 81.5 us -> 79.6 us  [shards(): pl.pallas_call(functools.partial(kernel, p), out_shape=(jax.ShapeDtypeStr...]
where the time goes in v3:
time: 83.4 us; the launch traced here: 83.2 us
  Pallas kernels  79.6 us (95%)
  local copies, waits for them, and re-layouts  2.97 us (4%)
    pallas_call x1, Pallas kernels, shards(): pl.pallas_call(functools.partial(kernel, p), out_shape=(jax.ShapeDtypeStr...  79.6 us
    unnamed x2, local copies, waits for them, and re-layouts  2.97 us

profile of v3, /device:TPU:0, one launch (start us, length us, event | category | flops | bytes accessed | tf_op | source)
XLA Modules:
  0.0 83.2 jit_solution(17173625950422946455)
XLA Ops:
  0.6 79.6 %gather_project_score.1 = (bf16[512,512]{1,0:T(8,128)(2,1)}, f32[2]{0:T(128)}) custom-call(bf16[512,4096]{1,0:T(8,128)(2,1)} %tok_hbm.1, bf16[512,1024]{1,0:T(8,128)(2,1)} %w_hbm.1, bf16[512,512]{1,0:T(8,128)(2,1)} %bitcast.5, bf16[64,512]{1,0:T(8,128)(2,1)} %bitcast.6, f32[1,512]{1,0:T(1,128)} %bitcast.7, s32[4]{0:T(128)} %tile_adapter.1, s32[8]{0:T(128)} %storage.1, ...), custom_call_target="tpu_custom_call" | custom-call | tf_op jit(solution)/shard_map/gather_project_score/pallas_call | solution.py:490
  80.2 1.9 %copy.14 = bf16[512,512]{1,0:T(8,128)(2,1)} copy(bf16[512,512]{1,0:T(8,128)(2,1)} %get-tuple-element.4) | data formatting | bytes 1048576
  82.1 1.1 %copy.15 = f32[2]{0:T(128)} copy(f32[2]{0:T(128)} %get-tuple-element.5) | data formatting | bytes 16
